TPU v7x, 32 devices: a whole 2x2x4 slice. The times are simulated.
32 devices in a mesh: groups: 2 (over y), seq: 16 (over z, x, core).
Axes of the slice: x: 2, y: 2, z: 4, core: 2. Of those that a mesh axis runs over, the one named last changes fastest.
Arguments:
- queries: bfloat16 [8192, 2048], P(('groups', 'seq')), parts along dimension 0, may hold values from -6 to 6
- key_inputs: bfloat16 [8192, 2048], P(('groups', 'seq')), parts along dimension 0, may hold values from -6 to 6
- values: bfloat16 [8192, 2048], P(('groups', 'seq')), parts along dimension 0, may hold values from -6 to 6
- short_taps: float32 [3, 3, 2048], replicated, may hold values from -3.6 to 3.6
- decay_rates: float32 [2, 2048], replicated, may hold values from 2.4414063e-05 to 0.05, as said below
- residues: float32 [2, 2048], replicated, may hold values from -6 to 6
- skip_gain: float32 [2048], replicated, may hold values from -6 to 6
- out_weight: bfloat16 [2048, 4096], P('seq'), may hold values from -0.125 to 0.125
- cotangent: bfloat16 [8192, 4096], P(('groups', 'seq')), parts along dimension 0, may hold values from -6 to 6
- doc_blocks: int32 [8], P('groups'), parts along dimension 0, may hold values from 1 to 16, 32 in all
Outputs:
- mixed_out: bfloat16 [8192, 4096], P(('groups', 'seq')), parts along dimension 0
- grad_queries: bfloat16 [8192, 2048], P(('groups', 'seq')), parts along dimension 0
- grad_keys: bfloat16 [8192, 2048], P(('groups', 'seq')), parts along dimension 0
- grad_values: bfloat16 [8192, 2048], P(('groups', 'seq')), parts along dimension 0
There are 2 independent parts, one for each index of `groups`. A program takes and returns all parts, laid end to end along the dimension named above; an argument that names none is the same for every part. Nothing has to cross between parts.
Inputs may be any that keep to these rules, and one draw needn't show every extreme that they name: `doc_blocks`: documents fill the batch in order: the entries sum to 32, and the longest is exactly 16 blocks. `decay_rates`: positive decay rates.
All inputs are finite; a program needn't handle non-finite values.
Results may differ from a plain program's by a relative error of at most 0.0051.
Values may be sent and summed in bfloat16 or wider, within the bound.
A program may use at most 128 MiB of HBM per device.

v0:
```python
import jax
import jax.numpy as jnp
from jax import lax
from jax.sharding import PartitionSpec as P

BLOCK = 128
exact_mode = lax.Precision.HIGHEST


def from_behind(value, axis, steps):
    count = lax.axis_size(axis)
    leading, last = (max(0, -steps), min(count, count - steps))
    return lax.ppermute(value, axis, [(source, source + steps) for source in range(leading, last)])


def combine(earlier, later):
    return (earlier[0] * later[0], later[0] * earlier[1] + later[1])


def block_marks(doc_blocks, first_block, block_count):
    doc_ends = jnp.cumsum(doc_blocks)
    starts = doc_ends - doc_blocks
    block_index = first_block + jnp.arange(block_count, dtype=jnp.int32)
    matches = (block_index[:, None] == starts[None, :]) | (block_index[:, None] >= doc_ends[-1])
    return jnp.any(matches, axis=1).astype(jnp.float32)


def block_parts(blocked, decay_rates, reset_flags):
    span = blocked.shape[-1]
    offsets = jnp.arange(span, dtype=jnp.float32)
    upper_ones = (offsets[:, None] <= offsets[None, :]).astype(jnp.float32)
    growth = jnp.exp(decay_rates[:, :, None] * offsets[None, None, :])
    shrink = jnp.exp(-decay_rates[:, :, None] * offsets[None, None, :])
    lifted = blocked[None, :, :, :] * growth[:, :, None, :]
    inside = (
        jnp.einsum("sgbp,pt->sgbt", lifted, upper_ones, precision=exact_mode)
        * shrink[:, :, None, :]
    )
    keep_rate = (1.0 - reset_flags)[None, None, :] * jnp.exp(-decay_rates * span)[:, :, None]
    cum_keep, cum_ends = lax.associative_scan(combine, (keep_rate, inside[..., -1]), axis=2)
    return (inside, cum_keep, cum_ends)


def block_finish(inside, cum_keep, cum_ends, decay_rates, filter_weight, reset_flags, incoming):
    span = inside.shape[-1]
    at_end = cum_keep * incoming[:, :, None] + cum_ends
    before = (
        jnp.concatenate([incoming[:, :, None], at_end[:, :, :-1]], axis=2)
        * (1.0 - reset_flags)[None, None, :]
    )
    offsets = jnp.arange(1, span + 1, dtype=jnp.float32)
    decay_rows = jnp.exp(-decay_rates[:, :, None] * offsets[None, None, :])
    summed_up = inside + before[..., None] * decay_rows[:, :, None, :]
    return jnp.sum(summed_up * filter_weight[:, :, None, None], axis=0)


def relay_pass(columns, decay_rates, filter_weight, doc_blocks, backward):
    device_place = lax.axis_index("seq")
    spread = lax.all_to_all(columns, "seq", split_axis=0, concat_axis=1, tiled=True)
    share_width = spread.shape[0]
    block_count = spread.shape[1] // BLOCK
    own_rates = lax.dynamic_slice_in_dim(decay_rates, device_place * share_width, share_width, 1)
    own_weights = lax.dynamic_slice_in_dim(
        filter_weight, device_place * share_width, share_width, 1
    )
    lead_shift = 1 if backward else 0
    reset_flags = block_marks(doc_blocks, lead_shift, block_count)
    blocked = spread.reshape(share_width, block_count, BLOCK)
    if backward:
        blocked = jnp.flip(blocked, axis=(1, 2))
        reset_flags = jnp.flip(reset_flags, axis=0)
    inside, cum_keep, cum_ends = block_parts(blocked, own_rates, reset_flags)
    zero_state = jnp.zeros(own_rates.shape, jnp.float32)
    result = block_finish(
        inside, cum_keep, cum_ends, own_rates, own_weights, reset_flags, zero_state
    )
    if backward:
        result = jnp.flip(result, axis=(1, 2))
    return lax.all_to_all(
        result.reshape(share_width, block_count * BLOCK),
        "seq",
        split_axis=1,
        concat_axis=0,
        tiled=True,
    )


def long_conv(columns, decay_rates, filter_weight, doc_blocks, backward):
    return relay_pass(columns, decay_rates, filter_weight, doc_blocks, backward)


def on_device(
    queries,
    key_inputs,
    values,
    short_taps,
    decay_rates,
    residues,
    skip_gain,
    out_weight,
    cotangent,
    doc_blocks,
):
    row_count = queries.shape[0]
    block_count = row_count // BLOCK
    marks_ext = block_marks(doc_blocks, lax.axis_index("seq") * block_count, block_count + 1)
    head_mask = (jnp.arange(BLOCK) == 0).astype(jnp.float32)
    begins = (marks_ext[:, None] * head_mask[None, :]).reshape(-1)[: row_count + 2]
    now_start = begins[:row_count]
    prior_start = jnp.concatenate([jnp.zeros((1,), jnp.float32), now_start[:-1]])
    keep_one = (1.0 - now_start)[:, None]
    keep_two = keep_one * (1.0 - prior_start)[:, None]
    next_one = (1.0 - begins[1 : row_count + 1])[:, None]
    next_two = next_one * (1.0 - begins[2 : row_count + 2])[:, None]
    tail_rows = jnp.stack(
        [queries[row_count - 2 :], key_inputs[row_count - 2 :], values[row_count - 2 :]]
    )
    prev_rims = from_behind(tail_rows, "seq", 1)

    def forward_short(current, rim_rows, tap_row):
        longer = jnp.concatenate([rim_rows, current], axis=0).astype(jnp.float32)
        return (
            tap_row[0] * longer[2:]
            + tap_row[1] * keep_one * longer[1:-1]
            + tap_row[2] * keep_two * longer[:-2]
        )

    q_short = forward_short(queries, prev_rims[0], short_taps[0])
    k_short = forward_short(key_inputs, prev_rims[1], short_taps[1])
    v_short = forward_short(values, prev_rims[2], short_taps[2])
    product = k_short * v_short
    filter_weight = residues * jnp.sqrt(2.0 * decay_rates)
    conv_out = (
        long_conv(product.T, decay_rates, filter_weight, doc_blocks, False).T + skip_gain * product
    )
    gated_rows = (q_short * conv_out).astype(jnp.bfloat16)
    weight_piece = lax.all_gather(out_weight, "seq", axis=0, tiled=True)
    total_out = jnp.dot(gated_rows, weight_piece, preferred_element_type=jnp.float32)
    column = lax.dot_general(
        cotangent, weight_piece, (((1,), (1,)), ((), ())), preferred_element_type=jnp.float32
    )
    total_out, grad_gated = (total_out, column)
    mixed_out = total_out.astype(jnp.bfloat16)
    grad_qs = grad_gated * conv_out
    grad_conv = grad_gated * q_short
    grad_product = (
        long_conv(grad_conv.T, decay_rates, filter_weight, doc_blocks, True).T
        + skip_gain * grad_conv
    )
    grad_ks = grad_product * v_short
    grad_vs = grad_product * k_short
    head_rows = jnp.stack([grad_qs[:2], grad_ks[:2], grad_vs[:2]])
    next_rims = from_behind(head_rows.astype(jnp.bfloat16), "seq", -1).astype(head_rows.dtype)

    def backward_short(gradient, rim_rows, tap_row):
        longer = jnp.concatenate([gradient, rim_rows], axis=0)
        summed = (
            tap_row[0] * gradient
            + tap_row[1] * next_one * longer[1 : row_count + 1]
            + tap_row[2] * next_two * longer[2:]
        )
        return summed.astype(jnp.bfloat16)

    grad_queries = backward_short(grad_qs, next_rims[0], short_taps[0])
    grad_keys = backward_short(grad_ks, next_rims[1], short_taps[1])
    grad_values = backward_short(grad_vs, next_rims[2], short_taps[2])
    return (mixed_out, grad_queries, grad_keys, grad_values)


def solution(mesh):
    return jax.shard_map(
        on_device,
        mesh=mesh,
        in_specs=(
            P(("groups", "seq"), None),
            P(("groups", "seq"), None),
            P(("groups", "seq"), None),
            P(),
            P(),
            P(),
            P(),
            P("seq", None),
            P(("groups", "seq"), None),
            P("groups"),
        ),
        out_specs=(
            P(("groups", "seq"), None),
            P(("groups", "seq"), None),
            P(("groups", "seq"), None),
            P(("groups", "seq"), None),
        ),
        check_vma=False,
    )
```

profile of v0, /device:TPU:16, one launch (start us, length us, event | category | flops | bytes accessed | tf_op | source)
XLA Modules:
  0.0 414.4 jit_solution(16186817507365080882)
XLA Ops:
  7.2 0.7 all-gather.2.cloned.1.call-update
  7.9 0.8 slice_bitcast_fusion.8
  8.7 0.8 slice_bitcast_fusion.6
  9.6 1.9 collective-permute-start
  11.5 0.8 reduce-window.4
  12.9 0.7 broadcast_compare_fusion.1
  13.6 0.7 bitcast_subtract_fusion
  14.5 0.7 fusion.63
  15.2 1.6 fusion.71
  16.9 0.6 slice_bitcast_fusion.4
  18.2 3.1 multiply_bitcast_fusion.1
  21.4 1.5 copy.42
  22.9 6.6 %all-to-all-start = ((f32[16,128,256]{1,2,0:T(8,128)}), f32[16,128,256]{1,2,0:T(8,128)}, u32[]{:S(2)}, u32[]{:S(2)}) async-start(f32[16,128,256]{1,2,0:T(8,128)} %bitcast.121), calls=%async_computation | async-start | bytes 4194304 | tf_op jit(solution)/shard_map/all_to_all | solution.py:59
  29.5 0.7 iota_compare_fusion.2
  30.3 1.3 dynamic-slice_multiply_fusion
  32.9 0.6 slice.510
  33.5 0.6 slice.491
  34.1 0.6 slice.490
  35.3 0.6 slice.558
  35.9 0.6 slice.539
  36.5 0.6 slice.538
  37.2 0.8 multiply_exponential_fusion
  38.0 2.5 maximum_convert_fusion
  40.5 68.7 %all-to-all-done = f32[16,128,256]{1,2,0:T(8,128)} async-done(((f32[16,128,256]{1,2,0:T(8,128)}), f32[16,128,256]{1,2,0:T(8,128)}, u32[]{:S(2)}, u32[]{:S(2)}) %all-to-all-start) | async-done | bytes 2097184 | tf_op jit(solution)/shard_map/all_to_all | solution.py:59
  109.2 2.9 copy.23
  112.2 60.0 %all-gather.2.cloned.1.call-done = bf16[2048,4096]{1,0:T(8,128)(2,1)} async-done(((bf16[128,4096]{1,0:T(8,128)(2,1)}), bf16[2048,4096]{1,0:T(8,128)(2,1)}) %all-gather.2.cloned.1.call-update) | async-done | bytes 16777232 | tf_op jit(solution)/shard_map/all_gather | solution.py:137
  172.2 9.5 %fusion.82 = f32[256,2048]{1,0:T(8,128)} fusion(bf16[256,4096]{1,0:T(8,128)(2,1)S(1)} %copy-done, bf16[2048,4096]{1,0:T(8,128)(2,1)} %all-gather.2.cloned.1.call-done), kind=kOutput, calls=%fused_computation.202 | convolution fusion | flops 4294967296 | bytes 20971520 | tf_op jit(solution)/shard_map/dot_general | solution.py:139
  181.7 6.8 %multiply_bitcast_fusion = (f32[32,16,8,128]{3,2,1,0:T(8,128)S(1)}, f32[256,2048]{1,0:T(8,128)}) fusion(f32[256,2048]{1,0:T(8,128)} %fusion.82, f32[258,2048]{1,0:T(8,128)} %maximum_convert_fusion, f32[256]{0:T(256)S(1)} %copy-done.30, f32[2048]{0:T(1024)S(1)} %bitcast.143, f32[256]{0:T(256)S(1)} %copy-done.28, f32[2048]{0:T(1024)S(1)} %bitcast.145, ...), kind=kLoop, calls=%fused_computation.65 | loop fusion | flops 4194304 | bytes 12609536
  188.4 1.5 copy.41
  190.0 6.7 %all-to-all-start.2 = ((f32[16,128,256]{1,2,0:T(8,128)}), f32[16,128,256]{1,2,0:T(8,128)}, u32[]{:S(2)}, u32[]{:S(2)}) async-start(f32[16,128,256]{1,2,0:T(8,128)} %bitcast.120), calls=%async_computation.2 | async-start | bytes 4194304 | tf_op jit(solution)/shard_map/all_to_all | solution.py:59
  196.7 2.8 fusion.4
  199.6 2.0 copy-done.4
  202.9 41.5 %all-to-all-done.2 = f32[16,128,256]{1,2,0:T(8,128)} async-done(((f32[16,128,256]{1,2,0:T(8,128)}), f32[16,128,256]{1,2,0:T(8,128)}, u32[]{:S(2)}, u32[]{:S(2)}) %all-to-all-start.2) | async-done | bytes 2097184 | tf_op jit(solution)/shard_map/all_to_all | solution.py:59
  244.4 16.5 %rev.11 = f32[128,32,128]{0,2,1:T(8,128)} reverse(f32[128,32,128]{0,2,1:T(8,128)} %bitcast.32), dimensions={1,2} | reverse | bytes 4194304 | tf_op jit(solution)/shard_map/jit(_flip)/rev | solution.py:70
  260.9 1.9 copy.27
  262.9 2.8 fusion.7
  265.8 2.0 copy-done.5
  269.1 6.8 %multiply_reduce_fusion = (f32[128,32,128]{0,2,1:T(8,128)S(1)}, f32[128,32,128]{0,2,1:T(8,128)}) fusion(f32[2,128,32,128]{1,3,2,0:T(8,128)} %copy-done.5, f32[2,128,32]{1,2,0:T(8,128)S(1)} %pad_multiply_fusion, f32[2,128]{1,0:T(2,128)S(1)} %copy-done.33, f32[2,128,128]{1,2,0:T(8,128)S(1)} %get-tuple-element.90, f32[2,128,32,128]{1,3,2,0:T(8,128)} %copy-done.4, ...), kind=kLoop, calls=%fused_computation.1 | loop fusion | flops 7340032 | bytes 12780544 | tf_op jit(solution)/shard_map/reduce_sum | solution.py:54
  275.9 4.7 %all-to-all-start.1 = ((f32[128,16,256]{0,2,1:T(8,128)}), f32[128,16,256]{0,2,1:T(8,128)}, u32[]{:S(2)}, u32[]{:S(2)}) async-start(f32[128,16,256]{0,2,1:T(8,128)} %bitcast.119), calls=%async_computation.1 | async-start | bytes 4194304 | tf_op jit(solution)/shard_map/all_to_all | solution.py:79
  280.6 10.3 %rev.13 = f32[128,32,128]{0,2,1:T(8,128)} reverse(f32[128,32,128]{0,2,1:T(8,128)S(1)} %get-tuple-element.4), dimensions={1,2} | reverse | bytes 4194304 | tf_op jit(solution)/shard_map/jit(_flip)/rev | solution.py:78
  290.9 37.5 %all-to-all-done.1 = f32[128,16,256]{0,2,1:T(8,128)} async-done(((f32[128,16,256]{0,2,1:T(8,128)}), f32[128,16,256]{0,2,1:T(8,128)}, u32[]{:S(2)}, u32[]{:S(2)}) %all-to-all-start.1) | async-done | bytes 2097184 | tf_op jit(solution)/shard_map/all_to_all | solution.py:79
  328.4 4.8 %all-to-all-start.3 = ((f32[128,16,256]{0,2,1:T(8,128)}), f32[128,16,256]{0,2,1:T(8,128)}, u32[]{:S(2)}, u32[]{:S(2)}) async-start(f32[128,16,256]{0,2,1:T(8,128)} %bitcast.122), calls=%async_computation.3 | async-start | bytes 4194304 | tf_op jit(solution)/shard_map/all_to_all | solution.py:79
  333.3 47.7 %all-to-all-done.3 = f32[128,16,256]{0,2,1:T(8,128)} async-done(((f32[128,16,256]{0,2,1:T(8,128)}), f32[128,16,256]{0,2,1:T(8,128)}, u32[]{:S(2)}, u32[]{:S(2)}) %all-to-all-start.3) | async-done | bytes 2097184 | tf_op jit(solution)/shard_map/all_to_all | solution.py:79
  380.9 5.2 %fusion.64 = (f32[256,2048]{1,0:T(8,128)S(1)}, f32[256,2048]{1,0:T(8,128)S(1)}, f32[256,2048]{1,0:T(8,128)S(1)}, f32[256,2048]{1,0:T(8,128)S(1)}) fusion(f32[256,2048]{1,0:T(8,128)} %get-tuple-element.13, f32[256,2048]{1,0:T(8,128)} %fusion.82, f32[256,2048]{1,0:T(8,128)} %get-tuple-element.18, f32[2048]{0:T(1024)S(1)} %copy-done.31, ...), kind=kLoop, calls=%fused_computation.189 | loop fusion | flops 4194304 | bytes 20979712 | tf_op jit(solution)/shard_map/mul | solution.py:150
  386.6 3.2 collective-permute-start.1
  389.8 11.6 %convolution_convert_fusion = bf16[256,4096]{1,0:T(8,128)(2,1)} fusion(bf16[2048,4096]{1,0:T(8,128)(2,1)} %all-gather.2.cloned.1.call-done, f32[256,2048]{1,0:T(8,128)S(1)} %copy-done.6, f32[256,2048]{1,0:T(8,128)S(1)} %get-tuple-element.20), kind=kOutput, calls=%fused_computation | convolution fusion | flops 4297064448 | bytes 23068672 | tf_op jit(solution)/shard_map/dot_general | solution.py:138
  401.5 1.9 fusion.24
  403.4 4.2 %fusion.14 = (bf16[256,2048]{1,0:T(8,128)(2,1)}, bf16[256,2048]{1,0:T(8,128)(2,1)}) fusion(f32[256,2048]{1,0:T(8,128)S(1)} %mul.732, f32[2,2048]{1,0:T(2,128)S(1)} %get-tuple-element.30, f32[256]{0:T(256)S(1)} %get-tuple-element.71, f32[256]{0:T(256)S(1)} %get-tuple-element.70, f32[2048]{0:T(1024)S(1)} %bitcast.140, f32[2048]{0:T(1024)S(1)} %bitcast.142, ...), kind=kLoop, calls=%fused_computation.19 | loop fusion | flops 10485760 | bytes 6375424 | tf_op jit(solution)/shard_map/convert_element_type | solution.py:162
  (247 shorter events, 6.3 us)
Async XLA Ops:
  7.2 165.0 %copy-start = (bf16[256,4096]{1,0:T(8,128)(2,1)S(1)}, bf16[256,4096]{1,0:T(8,128)(2,1)}, u32[]{:S(2)}) copy-start(bf16[256,4096]{1,0:T(8,128)(2,1)} %param.18) | copy-start | bytes 6291460
  7.2 10.4 %copy-start.7 = (bf16[256,2048]{1,0:T(8,128)(2,1)S(1)}, bf16[256,2048]{1,0:T(8,128)(2,1)}, u32[]{:S(2)}) copy-start(bf16[256,2048]{1,0:T(8,128)(2,1)} %param.11) | copy-start | bytes 3145732
  7.2 165.0 %all-gather.2.cloned.1.call-start = ((), (), s32[]{:S(2)}) async-start(), calls=%async_computation.4 | async-start | bytes 17825792 | tf_op jit(solution)/shard_map/all_gather | solution.py:137
  9.6 7.4 %collective-permute-start = (bf16[3,2,2048]{2,1,0:T(2,128)(2,1)S(1)}, bf16[3,2,2048]{2,1,0:T(2,128)(2,1)S(1)}, u32[]{:S(2)}, u32[]{:S(2)}) collective-permute-start(bf16[3,2,2048]{2,1,0:T(2,128)(2,1)S(1)} %pad_maximum_fusion.3), channel_id=1, source_target_pairs={{0,1},{1,2},{2,3},{3,4},{4,5},{5,6},{6,7},{7,8},{8,9},{9,10},{10,1... | collective-permute-start | bytes 73736 | tf_op jit(solution)/shard_map/ppermute | solution.py:13
  12.9 4.9 %copy-start.8 = (bf16[256,2048]{1,0:T(8,128)(2,1)S(1)}, bf16[256,2048]{1,0:T(8,128)(2,1)}, u32[]{:S(2)}) copy-start(bf16[256,2048]{1,0:T(8,128)(2,1)} %param.12) | copy-start | bytes 3145732
  16.8 1.4 copy-start.10
  16.8 1.4 copy-start.12
  16.8 1.4 copy-start.14
  16.8 1.4 copy-start.16
  16.9 1.3 copy-start.27
  16.9 1.3 copy-start.29
  22.9 15.1 %copy-start.9 = (bf16[256,2048]{1,0:T(8,128)(2,1)S(1)}, bf16[256,2048]{1,0:T(8,128)(2,1)}, u32[]{:S(2)}) copy-start(bf16[256,2048]{1,0:T(8,128)(2,1)} %param.10) | copy-start | bytes 3145732
  22.9 86.3 %all-to-all-start = ((f32[16,128,256]{1,2,0:T(8,128)}), f32[16,128,256]{1,2,0:T(8,128)}, u32[]{:S(2)}, u32[]{:S(2)}) async-start(f32[16,128,256]{1,2,0:T(8,128)} %bitcast.121), calls=%async_computation | async-start | bytes 4194304 | tf_op jit(solution)/shard_map/all_to_all | solution.py:59
  31.6 5.5 %copy-start.36 = (f32[32]{0:T(128)}, f32[32]{0:T(128)S(1)}, u32[]{:S(2)}) copy-start(f32[32]{0:T(128)S(1)} %broadcast_subtract_fusion.1) | copy-start | bytes 388
  31.6 5.5 %copy-start.38 = (f32[32]{0:T(128)}, f32[32]{0:T(128)S(1)}, u32[]{:S(2)}) copy-start(f32[32]{0:T(128)S(1)} %convert_subtract_fusion) | copy-start | bytes 388
  112.1 69.5 %copy-start.18 = (f32[1,1,2048]{2,1,0:T(1,128)S(1)}, f32[1,1,2048]{2,1,0:T(1,128)}, u32[]{:S(2)}) copy-start(f32[1,1,2048]{2,1,0:T(1,128)} %get-tuple-element.25) | copy-start | bytes 24580
  112.1 69.5 %copy-start.19 = (f32[1,1,2048]{2,1,0:T(1,128)S(1)}, f32[1,1,2048]{2,1,0:T(1,128)}, u32[]{:S(2)}) copy-start(f32[1,1,2048]{2,1,0:T(1,128)} %get-tuple-element.26) | copy-start | bytes 24580
  112.1 69.5 %copy-start.20 = (f32[1,1,2048]{2,1,0:T(1,128)S(1)}, f32[1,1,2048]{2,1,0:T(1,128)}, u32[]{:S(2)}) copy-start(f32[1,1,2048]{2,1,0:T(1,128)} %get-tuple-element.27) | copy-start | bytes 24580
  112.1 69.5 %copy-start.28 = (f32[256]{0:T(256)S(1)}, f32[256]{0:T(256)}, u32[]{:S(2)}) copy-start(f32[256]{0:T(256)} %copy-done.27) | copy-start | bytes 3076
  112.1 69.5 %copy-start.30 = (f32[256]{0:T(256)S(1)}, f32[256]{0:T(256)}, u32[]{:S(2)}) copy-start(f32[256]{0:T(256)} %copy-done.29) | copy-start | bytes 3076
  190.0 6.7 %copy-start.2 = (f32[128,32,128]{2,0,1:T(8,128)S(1)}, f32[128,32,128]{2,0,1:T(8,128)}, u32[]{:S(2)}) copy-start(f32[128,32,128]{2,0,1:T(8,128)} %copy.23) | copy-start | bytes 6291460
  190.0 54.5 %all-to-all-start.2 = ((f32[16,128,256]{1,2,0:T(8,128)}), f32[16,128,256]{1,2,0:T(8,128)}, u32[]{:S(2)}, u32[]{:S(2)}) async-start(f32[16,128,256]{1,2,0:T(8,128)} %bitcast.120), calls=%async_computation.2 | async-start | bytes 4194304 | tf_op jit(solution)/shard_map/all_to_all | solution.py:59
  196.7 5.0 %copy-start.23 = (f32[2,128,16]{1,2,0:T(8,128)S(1)}, f32[2,128,16]{1,2,0:T(8,128)}, u32[]{:S(2)}) copy-start(f32[2,128,16]{1,2,0:T(8,128)} %slice.491) | copy-start | bytes 49156
  196.7 5.0 %copy-start.24 = (f32[2,128,16]{1,2,0:T(8,128)S(1)}, f32[2,128,16]{1,2,0:T(8,128)}, u32[]{:S(2)}) copy-start(f32[2,128,16]{1,2,0:T(8,128)} %slice.490) | copy-start | bytes 49156
  196.7 6.0 %copy-start.26 = (f32[2,128,15]{1,2,0:T(8,128)S(1)}, f32[2,128,15]{1,2,0:T(8,128)}, u32[]{:S(2)}) copy-start(f32[2,128,15]{1,2,0:T(8,128)} %slice.510) | copy-start | bytes 46084
  196.7 6.0 %copy-start.35 = (f32[2,128,1]{1,2,0:T(1,128)S(1)}, f32[2,128,1]{1,2,0:T(1,128)}, u32[]{:S(2)}) copy-start(f32[2,128,1]{1,2,0:T(1,128)} %slice.607) | copy-start | bytes 3076
  196.7 6.2 %copy-start.39 = (f32[32]{0:T(128)S(1)}, f32[32]{0:T(128)}, u32[]{:S(2)}) copy-start(f32[32]{0:T(128)} %copy-done.38) | copy-start | bytes 388
  199.5 2.1 copy-start.4
  262.9 5.0 %copy-start.21 = (f32[2,128,16]{1,2,0:T(8,128)S(1)}, f32[2,128,16]{1,2,0:T(8,128)}, u32[]{:S(2)}) copy-start(f32[2,128,16]{1,2,0:T(8,128)} %slice.539) | copy-start | bytes 49156
  262.9 5.0 %copy-start.22 = (f32[2,128,16]{1,2,0:T(8,128)S(1)}, f32[2,128,16]{1,2,0:T(8,128)}, u32[]{:S(2)}) copy-start(f32[2,128,16]{1,2,0:T(8,128)} %slice.538) | copy-start | bytes 49156
  262.9 6.0 %copy-start.25 = (f32[2,128,15]{1,2,0:T(8,128)S(1)}, f32[2,128,15]{1,2,0:T(8,128)}, u32[]{:S(2)}) copy-start(f32[2,128,15]{1,2,0:T(8,128)} %slice.558) | copy-start | bytes 46084
  262.9 6.0 %copy-start.34 = (f32[2,128,1]{1,2,0:T(1,128)S(1)}, f32[2,128,1]{1,2,0:T(1,128)}, u32[]{:S(2)}) copy-start(f32[2,128,1]{1,2,0:T(1,128)} %slice.639) | copy-start | bytes 3076
  262.9 6.1 %copy-start.37 = (f32[32]{0:T(128)S(1)}, f32[32]{0:T(128)}, u32[]{:S(2)}) copy-start(f32[32]{0:T(128)} %copy-done.36) | copy-start | bytes 388
  262.9 6.2 %copy-start.33 = (f32[2,128]{1,0:T(2,128)S(1)}, f32[2,128]{1,0:T(2,128)}, u32[]{:S(2)}) copy-start(f32[2,128]{1,0:T(2,128)} %get-tuple-element.15) | copy-start | bytes 3076
  265.8 2.0 copy-start.5
  275.9 52.4 %all-to-all-start.1 = ((f32[128,16,256]{0,2,1:T(8,128)}), f32[128,16,256]{0,2,1:T(8,128)}, u32[]{:S(2)}, u32[]{:S(2)}) async-start(f32[128,16,256]{0,2,1:T(8,128)} %bitcast.119), calls=%async_computation.1 | async-start | bytes 4194304 | tf_op jit(solution)/shard_map/all_to_all | solution.py:79
  328.4 4.8 %copy-start.32 = (f32[384]{0:T(512)S(1)}, f32[384]{0:T(512)}, u32[]{:S(2)}) copy-start(f32[384]{0:T(512)} %get-tuple-element.86) | copy-start | bytes 4612
  328.4 52.6 %copy-start.3 = (f32[256,2048]{1,0:T(8,128)S(1)}, f32[256,2048]{1,0:T(8,128)}, u32[]{:S(2)}) copy-start(f32[256,2048]{1,0:T(8,128)} %get-tuple-element.14) | copy-start | bytes 6291460
  328.4 52.6 %copy-start.31 = (f32[2048]{0:T(1024)S(1)}, f32[2048]{0:T(1024)}, u32[]{:S(2)}) copy-start(f32[2048]{0:T(1024)} %param.16) | copy-start | bytes 24580
  328.4 52.6 %all-to-all-start.3 = ((f32[128,16,256]{0,2,1:T(8,128)}), f32[128,16,256]{0,2,1:T(8,128)}, u32[]{:S(2)}, u32[]{:S(2)}) async-start(f32[128,16,256]{0,2,1:T(8,128)} %bitcast.122), calls=%async_computation.3 | async-start | bytes 4194304 | tf_op jit(solution)/shard_map/all_to_all | solution.py:79
  386.2 3.6 copy-start.6
  386.6 14.8 %collective-permute-start.1 = (bf16[3,2,2048]{2,1,0:T(2,128)(2,1)S(1)}, bf16[3,2,2048]{2,1,0:T(2,128)(2,1)S(1)}, u32[]{:S(2)}, u32[]{:S(2)}) collective-permute-start(bf16[3,2,2048]{2,1,0:T(2,128)(2,1)S(1)} %pad_maximum_fusion.4), channel_id=1, source_target_pairs={{1,0},{2,1},{3,2},{4,3},{5,4},{6,5},{7,6},{8,7},{9,8},{10,9},{11,1... | collective-permute-start | bytes 73736 | tf_op jit(solution)/shard_map/ppermute | solution.py:13
  401.4 2.0 copy-start.11
  401.4 2.0 copy-start.13
  401.4 2.0 copy-start.15
  401.4 2.0 copy-start.17
  403.4 4.2 %copy-start.1 = (bf16[256,4096]{1,0:T(8,128)(2,1)S(1)}, bf16[256,4096]{1,0:T(8,128)(2,1)}, u32[]{:S(2)}) copy-start(bf16[256,4096]{1,0:T(8,128)(2,1)} %param.18) | copy-start | bytes 6291460
Sparse Core Ops, SparseCore 0:
  10.2 161.9 all-gather.1
where the time goes:
time: 416 us; the launch traced here: 414 us
  waiting for transfers between devices  256 us (62%)
  local copies, waits for them, and re-layouts  49.7 us (12%)
  other arithmetic  38.9 us (9%)
  starting transfers between devices  28 us (7%)
  matrix products  26.6 us (6%)
  between operations  15.2 us (4%)
    all_to_all x2, waiting for transfers between devices, relay_pass(): lax.all_to_all(columns, 'seq', split_axis=0, concat_axis=1, tiled=True)  110 us
    all_to_all x2, waiting for transfers between devices, relay_pass(): lax.all_to_all(result.reshape(share_width, block_count * BLOCK), 'seq', s...  85.2 us
    all_gather x1, waiting for transfers between devices, on_device(): weight_piece = lax.all_gather(out_weight, 'seq', axis=0, tiled=True)  60 us
    rev x2, local copies, waits for them, and re-layouts, relay_pass(): blocked = jnp.flip(blocked, axis=(1, 2))  18.5 us
    all_to_all x2, starting transfers between devices, relay_pass(): lax.all_to_all(columns, 'seq', split_axis=0, concat_axis=1, tiled=True)  13.3 us
    dot_general x1, matrix products, on_device(): jnp.dot(gated_rows, weight_piece, preferred_element_type=jnp.float32)  11.6 us
    rev x1, local copies, waits for them, and re-layouts, relay_pass(): result = jnp.flip(result, axis=(1, 2))  10.3 us
    unnamed x2, other arithmetic  9.89 us
  transfers between devices with their start and end apart: 7, of which 5 were waited for; matrix products, arithmetic and copies ran while one was open for 13% of the time, Pallas kernels for 0%

commit v1 on v0

--- a/solution.py
+++ b/solution.py
@@ -5,6 +5,16 @@
 
 BLOCK = 128
 exact_mode = lax.Precision.HIGHEST
+
+
+def gather_by_hops(x, axis, dim):
+    size = lax.axis_size(axis)
+    held, pieces = (x, [x])
+    for _ in range(size - 1):
+        held = lax.ppermute(held, axis, [(i, (i + 1) % size) for i in range(size)])
+        pieces.insert(0, held)
+    line = jnp.concatenate(pieces, axis=dim)
+    return jnp.roll(line, (lax.axis_index(axis) + 1) * x.shape[dim], axis=dim)
 
 
 def from_behind(value, axis, steps):
@@ -134,7 +144,7 @@
         long_conv(product.T, decay_rates, filter_weight, doc_blocks, False).T + skip_gain * product
     )
     gated_rows = (q_short * conv_out).astype(jnp.bfloat16)
-    weight_piece = lax.all_gather(out_weight, "seq", axis=0, tiled=True)
+    weight_piece = gather_by_hops(out_weight, "seq", 0)
     total_out = jnp.dot(gated_rows, weight_piece, preferred_element_type=jnp.float32)
     column = lax.dot_general(
         cotangent, weight_piece, (((1,), (1,)), ((), ())), preferred_element_type=jnp.float32

time: 416 us -> 578 us (1.39)
  waiting for transfers between devices: 256 us -> 357 us
  local copies, waits for them, and re-layouts: 49.7 us -> 107 us
  starting transfers between devices: 28 us -> 45 us
  between operations: 15.2 us -> 1.91 us
    ppermute x0 -> x15, waiting for transfers between devices: none -> 231 us  [gather_by_hops(): held = lax.ppermute(held, axis, [(i, (i + 1) % size) for i in range(size)])]
    all_to_all x2, waiting for transfers between devices: 110 us -> 41.2 us  [relay_pass(): lax.all_to_all(columns, 'seq', split_axis=0, concat_axis=1, tiled=True)]
    all_gather x1 -> x0, waiting for transfers between devices: 60 us -> none  [on_device(): weight_piece = lax.all_gather(out_weight, 'seq', axis=0, tiled=True)]
    unnamed x84 -> x145, local copies, waits for them, and re-layouts: 4.31 us -> 60.8 us
    all_to_all x2, starting transfers between devices: 13.3 us -> 30 us  [relay_pass(): lax.all_to_all(columns, 'seq', split_axis=0, concat_axis=1, tiled=True)]
  transfers between devices with their start and end apart: 7 -> 21, of which waited for: 5 -> 17; matrix products, arithmetic and copies ran while one was open for 13% -> 10% of each run, Pallas kernels for 0% -> 0%
where the time goes in v1:
time: 578 us; the launch traced here: 575 us
  waiting for transfers between devices  357 us (62%)
  local copies, waits for them, and re-layouts  107 us (19%)
  starting transfers between devices  45 us (8%)
  other arithmetic  37.5 us (6%)
  matrix products  26.2 us (5%)
    ppermute x15, waiting for transfers between devices, gather_by_hops(): held = lax.ppermute(held, axis, [(i, (i + 1) % size) for i in range(size)])  231 us
    all_to_all x2, waiting for transfers between devices, relay_pass(): lax.all_to_all(result.reshape(share_width, block_count * BLOCK), 'seq', s...  85.2 us
    unnamed x145, local copies, waits for them, and re-layouts  60.8 us
    all_to_all x2, waiting for transfers between devices, relay_pass(): lax.all_to_all(columns, 'seq', split_axis=0, concat_axis=1, tiled=True)  41.2 us
    all_to_all x2, starting transfers between devices, relay_pass(): lax.all_to_all(columns, 'seq', split_axis=0, concat_axis=1, tiled=True)  30 us
    rev x2, local copies, waits for them, and re-layouts, relay_pass(): blocked = jnp.flip(blocked, axis=(1, 2))  18.4 us
    dot_general x1, matrix products, on_device(): jnp.dot(gated_rows, weight_piece, preferred_element_type=jnp.float32)  12.3 us
  transfers between devices with their start and end apart: 21, of which 17 were waited for; matrix products, arithmetic and copies ran while one was open for 10% of the time, Pallas kernels for 0%

profile of v1, /device:TPU:16, one launch (start us, length us, event | category | flops | bytes accessed | tf_op | source)
XLA Modules:
  0.0 575.4 jit_solution(17986462289365130516)
XLA Ops:
  0.7 15.3 %collective-permute-done.1 = bf16[128,4096]{1,0:T(8,128)(2,1)S(1)} collective-permute-done((bf16[128,4096]{1,0:T(8,128)(2,1)}, bf16[128,4096]{1,0:T(8,128)(2,1)S(1)}, u32[]{:S(2)}, u32[]{:S(2)}) %collective-permute-start.1) | collective-permute-done | bytes 1048608 | tf_op jit(solution)/shard_map/ppermute | solution.py:14
  16.0 15.1 %collective-permute-done.2 = bf16[128,4096]{1,0:T(8,128)(2,1)S(1)} collective-permute-done((bf16[128,4096]{1,0:T(8,128)(2,1)S(1)}, bf16[128,4096]{1,0:T(8,128)(2,1)S(1)}, u32[]{:S(2)}, u32[]{:S(2)}) %collective-permute-start.2) | collective-permute-done | bytes 1048608 | tf_op jit(solution)/shard_map/ppermute | solution.py:14
  32.2 15.1 %collective-permute-done.3 = bf16[128,4096]{1,0:T(8,128)(2,1)S(1)} collective-permute-done((bf16[128,4096]{1,0:T(8,128)(2,1)S(1)}, bf16[128,4096]{1,0:T(8,128)(2,1)S(1)}, u32[]{:S(2)}, u32[]{:S(2)}) %collective-permute-start.3) | collective-permute-done | bytes 1048608 | tf_op jit(solution)/shard_map/ppermute | solution.py:14
  48.3 15.1 %collective-permute-done.4 = bf16[128,4096]{1,0:T(8,128)(2,1)S(1)} collective-permute-done((bf16[128,4096]{1,0:T(8,128)(2,1)S(1)}, bf16[128,4096]{1,0:T(8,128)(2,1)S(1)}, u32[]{:S(2)}, u32[]{:S(2)}) %collective-permute-start.4) | collective-permute-done | bytes 1048608 | tf_op jit(solution)/shard_map/ppermute | solution.py:14
  64.4 15.1 %collective-permute-done.5 = bf16[128,4096]{1,0:T(8,128)(2,1)S(1)} collective-permute-done((bf16[128,4096]{1,0:T(8,128)(2,1)S(1)}, bf16[128,4096]{1,0:T(8,128)(2,1)S(1)}, u32[]{:S(2)}, u32[]{:S(2)}) %collective-permute-start.5) | collective-permute-done | bytes 1048608 | tf_op jit(solution)/shard_map/ppermute | solution.py:14
  80.5 15.1 %collective-permute-done.6 = bf16[128,4096]{1,0:T(8,128)(2,1)S(1)} collective-permute-done((bf16[128,4096]{1,0:T(8,128)(2,1)S(1)}, bf16[128,4096]{1,0:T(8,128)(2,1)S(1)}, u32[]{:S(2)}, u32[]{:S(2)}) %collective-permute-start.6) | collective-permute-done | bytes 1048608 | tf_op jit(solution)/shard_map/ppermute | solution.py:14
  96.6 15.1 %collective-permute-done.7 = bf16[128,4096]{1,0:T(8,128)(2,1)S(1)} collective-permute-done((bf16[128,4096]{1,0:T(8,128)(2,1)S(1)}, bf16[128,4096]{1,0:T(8,128)(2,1)S(1)}, u32[]{:S(2)}, u32[]{:S(2)}) %collective-permute-start.7) | collective-permute-done | bytes 1048608 | tf_op jit(solution)/shard_map/ppermute | solution.py:14
  113.5 14.4 %collective-permute-done.8 = bf16[128,4096]{1,0:T(8,128)(2,1)} collective-permute-done((bf16[128,4096]{1,0:T(8,128)(2,1)S(1)}, bf16[128,4096]{1,0:T(8,128)(2,1)}, u32[]{:S(2)}, u32[]{:S(2)}) %collective-permute-start.8) | collective-permute-done | bytes 1048608 | tf_op jit(solution)/shard_map/ppermute | solution.py:14
  133.6 9.7 %collective-permute-done.9 = bf16[128,4096]{1,0:T(8,128)(2,1)} collective-permute-done((bf16[128,4096]{1,0:T(8,128)(2,1)}, bf16[128,4096]{1,0:T(8,128)(2,1)}, u32[]{:S(2)}, u32[]{:S(2)}) %collective-permute-start.9) | collective-permute-done | bytes 1048608 | tf_op jit(solution)/shard_map/ppermute | solution.py:14
  145.8 12.8 %collective-permute-done.10 = bf16[128,4096]{1,0:T(8,128)(2,1)S(1)} collective-permute-done((bf16[128,4096]{1,0:T(8,128)(2,1)}, bf16[128,4096]{1,0:T(8,128)(2,1)S(1)}, u32[]{:S(2)}, u32[]{:S(2)}) %collective-permute-start.10) | collective-permute-done | bytes 1048608 | tf_op jit(solution)/shard_map/ppermute | solution.py:14
  161.4 12.5 %collective-permute-done.11 = bf16[128,4096]{1,0:T(8,128)(2,1)} collective-permute-done((bf16[128,4096]{1,0:T(8,128)(2,1)S(1)}, bf16[128,4096]{1,0:T(8,128)(2,1)}, u32[]{:S(2)}, u32[]{:S(2)}) %collective-permute-start.11) | collective-permute-done | bytes 1048608 | tf_op jit(solution)/shard_map/ppermute | solution.py:14
  173.9 3.2 multiply_bitcast_fusion.1
  178.7 25.4 %all-to-all-start = ((f32[16,128,256]{1,2,0:T(8,128)}), f32[16,128,256]{1,2,0:T(8,128)}, u32[]{:S(2)}, u32[]{:S(2)}) async-start(f32[16,128,256]{1,2,0:T(8,128)} %bitcast.121), calls=%async_computation | async-start | bytes 4194304 | tf_op jit(solution)/shard_map/all_to_all | solution.py:69
  204.2 58.9 %collective-permute-done.13 = bf16[128,4096]{1,0:T(8,128)(2,1)} collective-permute-done((bf16[128,4096]{1,0:T(8,128)(2,1)}, bf16[128,4096]{1,0:T(8,128)(2,1)}, u32[]{:S(2)}, u32[]{:S(2)}) %collective-permute-start.13) | collective-permute-done | bytes 1048608 | tf_op jit(solution)/shard_map/ppermute | solution.py:14
  265.9 12.7 %collective-permute-done.14 = bf16[128,4096]{1,0:T(8,128)(2,1)} collective-permute-done((bf16[128,4096]{1,0:T(8,128)(2,1)}, bf16[128,4096]{1,0:T(8,128)(2,1)}, u32[]{:S(2)}, u32[]{:S(2)}) %collective-permute-start.14) | collective-permute-done | bytes 1048608 | tf_op jit(solution)/shard_map/ppermute | solution.py:14
  284.3 2.9 maximum_convert_fusion
  287.1 2.9 copy.23
  290.1 3.9 collective-permute-done.15
  294.0 2.3 constant_dynamic-update-slice_fusion.31
  296.3 2.3 constant_dynamic-update-slice_fusion.30
  298.6 2.4 constant_dynamic-update-slice_fusion.29
  301.0 2.4 constant_dynamic-update-slice_fusion.28
  303.4 2.3 constant_dynamic-update-slice_fusion.27
  306.8 2.4 constant_dynamic-update-slice_fusion.25
  309.2 2.4 constant_dynamic-update-slice_fusion.24
  320.1 2.3 constant_dynamic-update-slice_fusion.15
  322.4 2.3 constant_dynamic-update-slice_fusion.14
  324.7 2.4 constant_dynamic-update-slice_fusion.13
  327.1 2.3 constant_dynamic-update-slice_fusion.12
  329.4 2.3 constant_dynamic-update-slice_fusion.11
  332.8 2.3 constant_dynamic-update-slice_fusion.9
  335.1 2.3 constant_dynamic-update-slice_fusion.8
  345.9 8.3 %fusion.11 = f32[256,2048]{1,0:T(8,128)S(1)} fusion(bf16[256,4096]{1,0:T(8,128)(2,1)S(1)} %copy-done, bf16[4096,4096]{1,0:T(8,128)(2,1)} %constant_dynamic-update-slice_fusion, s32[]{:T(128)S(6)} %select_n.21), kind=kOutput, calls=%fused_computation.11 | convolution fusion | flops 4294967296 | bytes 20971524 | tf_op jit(solution)/shard_map/dot_general | solution.py:149
  358.0 4.7 all-to-all-start.2
  362.7 2.8 fusion.14
  368.9 41.2 %all-to-all-done.2 = f32[16,128,256]{1,2,0:T(8,128)} async-done(((f32[16,128,256]{1,2,0:T(8,128)}), f32[16,128,256]{1,2,0:T(8,128)}, u32[]{:S(2)}, u32[]{:S(2)}) %all-to-all-start.2) | async-done | bytes 2097184 | tf_op jit(solution)/shard_map/all_to_all | solution.py:69
  410.1 16.5 %rev.11 = f32[128,32,128]{0,2,1:T(8,128)} reverse(f32[128,32,128]{0,2,1:T(8,128)} %bitcast.33), dimensions={1,2} | reverse | bytes 4194304 | tf_op jit(solution)/shard_map/jit(_flip)/rev | solution.py:80
  428.6 2.8 fusion.17
  434.7 6.9 %multiply_reduce_fusion = (f32[128,32,128]{0,2,1:T(8,128)S(1)}, f32[128,32,128]{0,2,1:T(8,128)}) fusion(f32[2,128,32,128]{1,3,2,0:T(8,128)} %copy-done.6, f32[2,128,32]{1,2,0:T(8,128)S(1)} %pad_multiply_fusion, f32[2,128]{1,0:T(2,128)S(1)} %copy-done.48, f32[2,128,128]{1,2,0:T(8,128)S(1)} %get-tuple-element.90, f32[2,128,32,128]{1,3,2,0:T(8,128)} %copy-done.5, ...), kind=kLoop, calls=%fused_computation.5 | loop fusion | flops 7340032 | bytes 12780544 | tf_op jit(solution)/shard_map/reduce_sum | solution.py:64
  441.6 4.7 all-to-all-start.1
  446.2 10.2 %rev.13 = f32[128,32,128]{0,2,1:T(8,128)} reverse(f32[128,32,128]{0,2,1:T(8,128)S(1)} %get-tuple-element.4), dimensions={1,2} | reverse | bytes 4194304 | tf_op jit(solution)/shard_map/jit(_flip)/rev | solution.py:88
  456.4 37.5 %all-to-all-done.1 = f32[128,16,256]{0,2,1:T(8,128)} async-done(((f32[128,16,256]{0,2,1:T(8,128)}), f32[128,16,256]{0,2,1:T(8,128)}, u32[]{:S(2)}, u32[]{:S(2)}) %all-to-all-start.1) | async-done | bytes 2097184 | tf_op jit(solution)/shard_map/all_to_all | solution.py:89
  494.0 4.8 all-to-all-start.3
  498.9 47.7 %all-to-all-done.3 = f32[128,16,256]{0,2,1:T(8,128)} async-done(((f32[128,16,256]{0,2,1:T(8,128)}), f32[128,16,256]{0,2,1:T(8,128)}, u32[]{:S(2)}, u32[]{:S(2)}) %all-to-all-start.3) | async-done | bytes 2097184 | tf_op jit(solution)/shard_map/all_to_all | solution.py:89
  546.6 6.7 %fusion.76 = (f32[256,2048]{1,0:T(8,128)S(1)}, f32[256,2048]{1,0:T(8,128)S(1)}, f32[256,2048]{1,0:T(8,128)S(1)}, f32[256,2048]{1,0:T(8,128)}) fusion(f32[256,2048]{1,0:T(8,128)} %get-tuple-element.13, f32[256,2048]{1,0:T(8,128)} %copy-done.8, f32[256,2048]{1,0:T(8,128)} %get-tuple-element.18, f32[2048]{0:T(1024)S(1)} %copy-done.46, ...), kind=kLoop, calls=%fused_computation.228 | loop fusion | flops 4194304 | bytes 20979712 | tf_op jit(solution)/shard_map/mul | solution.py:160
  553.6 3.2 collective-permute-start.16
  556.8 12.3 %fusion.4 = bf16[256,4096]{1,0:T(8,128)(2,1)} fusion(bf16[4096,4096]{1,0:T(8,128)(2,1)} %constant_dynamic-update-slice_fusion, s32[]{:T(128)S(6)} %select_n.21, f32[256,2048]{1,0:T(8,128)S(1)} %copy-done.7, f32[256,2048]{1,0:T(8,128)} %get-tuple-element.20), kind=kOutput, calls=%fused_computation.4 | convolution fusion | flops 4297064448 | bytes 23068676 | tf_op jit(solution)/shard_map/dot_general | solution.py:148
  571.2 4.2 fusion.24
  (336 shorter events, 60.9 us)
Async XLA Ops:
  0.6 345.2 %copy-start = (bf16[256,4096]{1,0:T(8,128)(2,1)S(1)}, bf16[256,4096]{1,0:T(8,128)(2,1)}, u32[]{:S(2)}) copy-start(bf16[256,4096]{1,0:T(8,128)(2,1)} %param.18) | copy-start | bytes 6291460
  0.6 15.4 %collective-permute-start.1 = (bf16[128,4096]{1,0:T(8,128)(2,1)}, bf16[128,4096]{1,0:T(8,128)(2,1)S(1)}, u32[]{:S(2)}, u32[]{:S(2)}) collective-permute-start(bf16[128,4096]{1,0:T(8,128)(2,1)} %param.17), channel_id=1, source_target_pairs={{0,1},{1,2},{2,3},{3,4},{4,5},{5,6},{6,7},{7,8},{8,9},{9,10},{10,1... | collective-permute-start | bytes 3145736 | tf_op jit(solution)/shard_map/ppermute | solution.py:14
  16.0 15.1 %collective-permute-start.2 = (bf16[128,4096]{1,0:T(8,128)(2,1)S(1)}, bf16[128,4096]{1,0:T(8,128)(2,1)S(1)}, u32[]{:S(2)}, u32[]{:S(2)}) collective-permute-start(bf16[128,4096]{1,0:T(8,128)(2,1)S(1)} %collective-permute-done.1), channel_id=1, source_target_pairs={{0,1},{1,2},{2,3},{3,4},{4,5},{5,6},{6,7},{7,8},{8,9},{9,10},{10,1... | collective-permute-start | bytes 3145736 | tf_op jit(solution)/shard_map/ppermute | solution.py:14
  32.2 15.1 %collective-permute-start.3 = (bf16[128,4096]{1,0:T(8,128)(2,1)S(1)}, bf16[128,4096]{1,0:T(8,128)(2,1)S(1)}, u32[]{:S(2)}, u32[]{:S(2)}) collective-permute-start(bf16[128,4096]{1,0:T(8,128)(2,1)S(1)} %collective-permute-done.2), channel_id=1, source_target_pairs={{0,1},{1,2},{2,3},{3,4},{4,5},{5,6},{6,7},{7,8},{8,9},{9,10},{10,1... | collective-permute-start | bytes 3145736 | tf_op jit(solution)/shard_map/ppermute | solution.py:14
  48.3 15.1 %collective-permute-start.4 = (bf16[128,4096]{1,0:T(8,128)(2,1)S(1)}, bf16[128,4096]{1,0:T(8,128)(2,1)S(1)}, u32[]{:S(2)}, u32[]{:S(2)}) collective-permute-start(bf16[128,4096]{1,0:T(8,128)(2,1)S(1)} %collective-permute-done.3), channel_id=1, source_target_pairs={{0,1},{1,2},{2,3},{3,4},{4,5},{5,6},{6,7},{7,8},{8,9},{9,10},{10,1... | collective-permute-start | bytes 3145736 | tf_op jit(solution)/shard_map/ppermute | solution.py:14
  64.4 15.1 %collective-permute-start.5 = (bf16[128,4096]{1,0:T(8,128)(2,1)S(1)}, bf16[128,4096]{1,0:T(8,128)(2,1)S(1)}, u32[]{:S(2)}, u32[]{:S(2)}) collective-permute-start(bf16[128,4096]{1,0:T(8,128)(2,1)S(1)} %collective-permute-done.4), channel_id=1, source_target_pairs={{0,1},{1,2},{2,3},{3,4},{4,5},{5,6},{6,7},{7,8},{8,9},{9,10},{10,1... | collective-permute-start | bytes 3145736 | tf_op jit(solution)/shard_map/ppermute | solution.py:14
  80.5 15.1 %collective-permute-start.6 = (bf16[128,4096]{1,0:T(8,128)(2,1)S(1)}, bf16[128,4096]{1,0:T(8,128)(2,1)S(1)}, u32[]{:S(2)}, u32[]{:S(2)}) collective-permute-start(bf16[128,4096]{1,0:T(8,128)(2,1)S(1)} %collective-permute-done.5), channel_id=1, source_target_pairs={{0,1},{1,2},{2,3},{3,4},{4,5},{5,6},{6,7},{7,8},{8,9},{9,10},{10,1... | collective-permute-start | bytes 3145736 | tf_op jit(solution)/shard_map/ppermute | solution.py:14
  96.6 15.1 %collective-permute-start.7 = (bf16[128,4096]{1,0:T(8,128)(2,1)S(1)}, bf16[128,4096]{1,0:T(8,128)(2,1)S(1)}, u32[]{:S(2)}, u32[]{:S(2)}) collective-permute-start(bf16[128,4096]{1,0:T(8,128)(2,1)S(1)} %collective-permute-done.6), channel_id=1, source_target_pairs={{0,1},{1,2},{2,3},{3,4},{4,5},{5,6},{6,7},{7,8},{8,9},{9,10},{10,1... | collective-permute-start | bytes 3145736 | tf_op jit(solution)/shard_map/ppermute | solution.py:14
  112.7 15.2 %collective-permute-start.8 = (bf16[128,4096]{1,0:T(8,128)(2,1)S(1)}, bf16[128,4096]{1,0:T(8,128)(2,1)}, u32[]{:S(2)}, u32[]{:S(2)}) collective-permute-start(bf16[128,4096]{1,0:T(8,128)(2,1)S(1)} %collective-permute-done.7), channel_id=1, source_target_pairs={{0,1},{1,2},{2,3},{3,4},{4,5},{5,6},{6,7},{7,8},{8,9},{9,10},{10,1... | collective-permute-start | bytes 3145736 | tf_op jit(solution)/shard_map/ppermute | solution.py:14
  127.9 15.4 %collective-permute-start.9 = (bf16[128,4096]{1,0:T(8,128)(2,1)}, bf16[128,4096]{1,0:T(8,128)(2,1)}, u32[]{:S(2)}, u32[]{:S(2)}) collective-permute-start(bf16[128,4096]{1,0:T(8,128)(2,1)} %collective-permute-done.8), channel_id=1, source_target_pairs={{0,1},{1,2},{2,3},{3,4},{4,5},{5,6},{6,7},{7,8},{8,9},{9,10},{10,1... | collective-permute-start | bytes 3145736 | tf_op jit(solution)/shard_map/ppermute | solution.py:14
  128.7 30.0 %collective-permute-start = (bf16[3,2,2048]{2,1,0:T(2,128)(2,1)S(1)}, bf16[3,2,2048]{2,1,0:T(2,128)(2,1)S(1)}, u32[]{:S(2)}, u32[]{:S(2)}) collective-permute-start(bf16[3,2,2048]{2,1,0:T(2,128)(2,1)S(1)} %pad_maximum_fusion.3), channel_id=1, source_target_pairs={{0,1},{1,2},{2,3},{3,4},{4,5},{5,6},{6,7},{7,8},{8,9},{9,10},{10,1... | collective-permute-start | bytes 73736 | tf_op jit(solution)/shard_map/ppermute | solution.py:23
  132.1 28.9 %copy-start.24 = (bf16[256,2048]{1,0:T(8,128)(2,1)S(1)}, bf16[256,2048]{1,0:T(8,128)(2,1)}, u32[]{:S(2)}) copy-start(bf16[256,2048]{1,0:T(8,128)(2,1)} %param.11) | copy-start | bytes 3145732
  143.3 15.3 %collective-permute-start.10 = (bf16[128,4096]{1,0:T(8,128)(2,1)}, bf16[128,4096]{1,0:T(8,128)(2,1)S(1)}, u32[]{:S(2)}, u32[]{:S(2)}) collective-permute-start(bf16[128,4096]{1,0:T(8,128)(2,1)} %collective-permute-done.9), channel_id=1, source_target_pairs={{0,1},{1,2},{2,3},{3,4},{4,5},{5,6},{6,7},{7,8},{8,9},{9,10},{10,1... | collective-permute-start | bytes 3145736 | tf_op jit(solution)/shard_map/ppermute | solution.py:14
  145.8 28.1 %copy-start.25 = (f32[1,1,2048]{2,1,0:T(1,128)}, f32[1,1,2048]{2,1,0:T(1,128)S(1)}, u32[]{:S(2)}) copy-start(f32[1,1,2048]{2,1,0:T(1,128)S(1)} %get-tuple-element.23) | copy-start | bytes 24580
  145.8 28.1 %copy-start.27 = (f32[1,1,2048]{2,1,0:T(1,128)}, f32[1,1,2048]{2,1,0:T(1,128)S(1)}, u32[]{:S(2)}) copy-start(f32[1,1,2048]{2,1,0:T(1,128)S(1)} %get-tuple-element.24) | copy-start | bytes 24580
  145.8 28.1 %copy-start.29 = (f32[1,1,2048]{2,1,0:T(1,128)}, f32[1,1,2048]{2,1,0:T(1,128)S(1)}, u32[]{:S(2)}) copy-start(f32[1,1,2048]{2,1,0:T(1,128)S(1)} %get-tuple-element.28) | copy-start | bytes 24580
  145.8 28.1 %copy-start.31 = (f32[1,1,2048]{2,1,0:T(1,128)}, f32[1,1,2048]{2,1,0:T(1,128)S(1)}, u32[]{:S(2)}) copy-start(f32[1,1,2048]{2,1,0:T(1,128)S(1)} %get-tuple-element.29) | copy-start | bytes 24580
  158.7 15.2 %collective-permute-start.11 = (bf16[128,4096]{1,0:T(8,128)(2,1)S(1)}, bf16[128,4096]{1,0:T(8,128)(2,1)}, u32[]{:S(2)}, u32[]{:S(2)}) collective-permute-start(bf16[128,4096]{1,0:T(8,128)(2,1)S(1)} %collective-permute-done.10), channel_id=1, source_target_pairs={{0,1},{1,2},{2,3},{3,4},{4,5},{5,6},{6,7},{7,8},{8,9},{9,10},{10,1... | collective-permute-start | bytes 3145736 | tf_op jit(solution)/shard_map/ppermute | solution.py:14
  158.7 15.2 %copy-start.42 = (f32[256]{0:T(256)}, f32[256]{0:T(256)S(1)}, u32[]{:S(2)}) copy-start(f32[256]{0:T(256)S(1)} %get-tuple-element.84) | copy-start | bytes 3076
  158.7 15.2 %copy-start.44 = (f32[256]{0:T(256)}, f32[256]{0:T(256)S(1)}, u32[]{:S(2)}) copy-start(f32[256]{0:T(256)S(1)} %get-tuple-element.85) | copy-start | bytes 3076
  173.9 30.1 %collective-permute-start.12 = (bf16[128,4096]{1,0:T(8,128)(2,1)}, bf16[128,4096]{1,0:T(8,128)(2,1)}, u32[]{:S(2)}, u32[]{:S(2)}) collective-permute-start(bf16[128,4096]{1,0:T(8,128)(2,1)} %collective-permute-done.11), channel_id=1, source_target_pairs={{0,1},{1,2},{2,3},{3,4},{4,5},{5,6},{6,7},{7,8},{8,9},{9,10},{10,1... | collective-permute-start | bytes 3145736 | tf_op jit(solution)/shard_map/ppermute | solution.py:14
  178.7 108.5 %all-to-all-start = ((f32[16,128,256]{1,2,0:T(8,128)}), f32[16,128,256]{1,2,0:T(8,128)}, u32[]{:S(2)}, u32[]{:S(2)}) async-start(f32[16,128,256]{1,2,0:T(8,128)} %bitcast.121), calls=%async_computation | async-start | bytes 4194304 | tf_op jit(solution)/shard_map/all_to_all | solution.py:69
  204.0 59.1 %collective-permute-start.13 = (bf16[128,4096]{1,0:T(8,128)(2,1)}, bf16[128,4096]{1,0:T(8,128)(2,1)}, u32[]{:S(2)}, u32[]{:S(2)}) collective-permute-start(bf16[128,4096]{1,0:T(8,128)(2,1)} %collective-permute-done.12), channel_id=1, source_target_pairs={{0,1},{1,2},{2,3},{3,4},{4,5},{5,6},{6,7},{7,8},{8,9},{9,10},{10,1... | collective-permute-start | bytes 3145736 | tf_op jit(solution)/shard_map/ppermute | solution.py:14
  263.1 15.4 %collective-permute-start.14 = (bf16[128,4096]{1,0:T(8,128)(2,1)}, bf16[128,4096]{1,0:T(8,128)(2,1)}, u32[]{:S(2)}, u32[]{:S(2)}) collective-permute-start(bf16[128,4096]{1,0:T(8,128)(2,1)} %collective-permute-done.13), channel_id=1, source_target_pairs={{0,1},{1,2},{2,3},{3,4},{4,5},{5,6},{6,7},{7,8},{8,9},{9,10},{10,1... | collective-permute-start | bytes 3145736 | tf_op jit(solution)/shard_map/ppermute | solution.py:14
  265.3 18.1 %copy-start.53 = (f32[32]{0:T(128)}, f32[32]{0:T(128)S(1)}, u32[]{:S(2)}) copy-start(f32[32]{0:T(128)S(1)} %convert_subtract_fusion) | copy-start | bytes 388
  265.3 18.1 %copy-start.51 = (f32[32]{0:T(128)}, f32[32]{0:T(128)S(1)}, u32[]{:S(2)}) copy-start(f32[32]{0:T(128)S(1)} %broadcast_subtract_fusion.1) | copy-start | bytes 388
  278.5 15.4 %collective-permute-start.15 = (bf16[128,4096]{1,0:T(8,128)(2,1)}, bf16[128,4096]{1,0:T(8,128)(2,1)}, u32[]{:S(2)}, u32[]{:S(2)}) collective-permute-start(bf16[128,4096]{1,0:T(8,128)(2,1)} %collective-permute-done.14), channel_id=1, source_target_pairs={{0,1},{1,2},{2,3},{3,4},{4,5},{5,6},{6,7},{7,8},{8,9},{9,10},{10,1... | collective-permute-start | bytes 3145736 | tf_op jit(solution)/shard_map/ppermute | solution.py:14
  345.8 8.4 %copy-start.2 = (f32[258,2048]{1,0:T(8,128)S(1)}, f32[258,2048]{1,0:T(8,128)}, u32[]{:S(2)}) copy-start(f32[258,2048]{1,0:T(8,128)} %maximum_convert_fusion) | copy-start | bytes 6340612
  345.8 8.4 %copy-start.33 = (f32[1,1,2048]{2,1,0:T(1,128)S(1)}, f32[1,1,2048]{2,1,0:T(1,128)}, u32[]{:S(2)}) copy-start(f32[1,1,2048]{2,1,0:T(1,128)} %get-tuple-element.25) | copy-start | bytes 24580
  345.8 8.4 %copy-start.34 = (f32[1,1,2048]{2,1,0:T(1,128)S(1)}, f32[1,1,2048]{2,1,0:T(1,128)}, u32[]{:S(2)}) copy-start(f32[1,1,2048]{2,1,0:T(1,128)} %get-tuple-element.26) | copy-start | bytes 24580
  345.8 8.4 %copy-start.35 = (f32[1,1,2048]{2,1,0:T(1,128)S(1)}, f32[1,1,2048]{2,1,0:T(1,128)}, u32[]{:S(2)}) copy-start(f32[1,1,2048]{2,1,0:T(1,128)} %get-tuple-element.27) | copy-start | bytes 24580
  345.8 8.4 %copy-start.43 = (f32[256]{0:T(256)S(1)}, f32[256]{0:T(256)}, u32[]{:S(2)}) copy-start(f32[256]{0:T(256)} %copy-done.42) | copy-start | bytes 3076
  345.8 8.4 %copy-start.45 = (f32[256]{0:T(256)S(1)}, f32[256]{0:T(256)}, u32[]{:S(2)}) copy-start(f32[256]{0:T(256)} %copy-done.44) | copy-start | bytes 3076
  358.0 52.1 %all-to-all-start.2 = ((f32[16,128,256]{1,2,0:T(8,128)}), f32[16,128,256]{1,2,0:T(8,128)}, u32[]{:S(2)}, u32[]{:S(2)}) async-start(f32[16,128,256]{1,2,0:T(8,128)} %bitcast.120), calls=%async_computation.2 | async-start | bytes 4194304 | tf_op jit(solution)/shard_map/all_to_all | solution.py:69
  362.7 4.9 copy-start.38
  362.7 4.9 copy-start.39
  362.7 5.9 %copy-start.41 = (f32[2,128,15]{1,2,0:T(8,128)S(1)}, f32[2,128,15]{1,2,0:T(8,128)}, u32[]{:S(2)}) copy-start(f32[2,128,15]{1,2,0:T(8,128)} %slice.510) | copy-start | bytes 46084
  362.7 6.0 %copy-start.50 = (f32[2,128,1]{1,2,0:T(1,128)S(1)}, f32[2,128,1]{1,2,0:T(1,128)}, u32[]{:S(2)}) copy-start(f32[2,128,1]{1,2,0:T(1,128)} %slice.607) | copy-start | bytes 3076
  362.7 6.1 %copy-start.54 = (f32[32]{0:T(128)S(1)}, f32[32]{0:T(128)}, u32[]{:S(2)}) copy-start(f32[32]{0:T(128)} %copy-done.53) | copy-start | bytes 388
  428.5 5.9 %copy-start.40 = (f32[2,128,15]{1,2,0:T(8,128)S(1)}, f32[2,128,15]{1,2,0:T(8,128)}, u32[]{:S(2)}) copy-start(f32[2,128,15]{1,2,0:T(8,128)} %slice.558) | copy-start | bytes 46084
  428.5 6.0 %copy-start.49 = (f32[2,128,1]{1,2,0:T(1,128)S(1)}, f32[2,128,1]{1,2,0:T(1,128)}, u32[]{:S(2)}) copy-start(f32[2,128,1]{1,2,0:T(1,128)} %slice.639) | copy-start | bytes 3076
  428.5 6.1 %copy-start.52 = (f32[32]{0:T(128)S(1)}, f32[32]{0:T(128)}, u32[]{:S(2)}) copy-start(f32[32]{0:T(128)} %copy-done.51) | copy-start | bytes 388
  428.6 6.1 %copy-start.48 = (f32[2,128]{1,0:T(2,128)S(1)}, f32[2,128]{1,0:T(2,128)}, u32[]{:S(2)}) copy-start(f32[2,128]{1,0:T(2,128)} %get-tuple-element.15) | copy-start | bytes 3076
  441.6 52.4 %all-to-all-start.1 = ((f32[128,16,256]{0,2,1:T(8,128)}), f32[128,16,256]{0,2,1:T(8,128)}, u32[]{:S(2)}, u32[]{:S(2)}) async-start(f32[128,16,256]{0,2,1:T(8,128)} %bitcast.119), calls=%async_computation.1 | async-start | bytes 4194304 | tf_op jit(solution)/shard_map/all_to_all | solution.py:89
  494.0 52.6 %copy-start.4 = (f32[256,2048]{1,0:T(8,128)S(1)}, f32[256,2048]{1,0:T(8,128)}, u32[]{:S(2)}) copy-start(f32[256,2048]{1,0:T(8,128)} %get-tuple-element.14) | copy-start | bytes 6291460
  494.0 52.6 %copy-start.46 = (f32[2048]{0:T(1024)S(1)}, f32[2048]{0:T(1024)}, u32[]{:S(2)}) copy-start(f32[2048]{0:T(1024)} %param.16) | copy-start | bytes 24580
  494.0 52.6 %all-to-all-start.3 = ((f32[128,16,256]{0,2,1:T(8,128)}), f32[128,16,256]{0,2,1:T(8,128)}, u32[]{:S(2)}, u32[]{:S(2)}) async-start(f32[128,16,256]{0,2,1:T(8,128)} %bitcast.122), calls=%async_computation.3 | async-start | bytes 4194304 | tf_op jit(solution)/shard_map/all_to_all | solution.py:89
  553.6 15.6 %collective-permute-start.16 = (bf16[3,2,2048]{2,1,0:T(2,128)(2,1)S(1)}, bf16[3,2,2048]{2,1,0:T(2,128)(2,1)S(1)}, u32[]{:S(2)}, u32[]{:S(2)}) collective-permute-start(bf16[3,2,2048]{2,1,0:T(2,128)(2,1)S(1)} %pad_maximum_fusion.4), channel_id=1, source_target_pairs={{1,0},{2,1},{3,2},{4,3},{5,4},{6,5},{7,6},{8,7},{9,8},{10,9},{11,1... | collective-permute-start | bytes 73736 | tf_op jit(solution)/shard_map/ppermute | solution.py:23
  (28 other events, 73.7 us)
